TPU v7x, 32 devices: a whole 2x2x4 slice. The times are simulated.
32 devices in a mesh: gy: 2 (over y), gx: 16 (over z, x, core).
Axes of the slice: x: 2, y: 2, z: 4, core: 2. Of those that a mesh axis runs over, the one named last changes fastest.
Arguments:
- feature_grid_cells: bfloat16 [32, 256, 768], P('gy', 'gx'), may hold values from -6 to 6
- triple_mapping_matrix: bfloat16 [2, 768, 2304], replicated, may hold values from -0.21875 to 0.21875
- asker_answer_shift: float32 [2, 2, 768], replicated, may hold values from -3 to 3
- cosine_sharpness: float32 [2, 24], replicated, may hold values from 4 to 40
- offset_mlp_entry_matrix: float32 [2, 2, 512], replicated, may hold values from -5 to 5
- offset_mlp_entry_shift: float32 [2, 512], replicated, may hold values from -3 to 3
- offset_mlp_exit_matrix: float32 [2, 512, 24], replicated, may hold values from -0.25 to 0.25
- mixing_matrix: bfloat16 [2, 768, 768], replicated, may hold values from -0.21875 to 0.21875
- mixing_shift_vector: float32 [2, 768], replicated, may hold values from -3 to 3
- rescaling_gain: float32 [2, 768], replicated, may hold values from 0.25 to 1.75
- rescaling_shift: float32 [2, 768], replicated, may hold values from -3 to 3
Outputs:
- mixed: bfloat16 [32, 256, 768], P('gy', 'gx')
All inputs are finite; a program needn't handle non-finite values.
Results may differ from a plain program's by a relative error of at most 0.0099.
Values may be sent and summed in bfloat16 or wider, within the bound.
A program may use at most 192 MiB of HBM per device.

v0:
```python
import functools

import jax
import jax.numpy as jnp
from jax import lax
from jax.experimental import pallas as pl
from jax.experimental.pallas import tpu as pltpu
from jax.sharding import PartitionSpec as P

HEADS = 24
WIN = 16
HALF = WIN // 2
TOKENS = WIN * WIN
QUARTER = HALF * HALF
HEAD_DIM = 32
PACK = 4
LANES = PACK * HEAD_DIM
SPAN = 2 * WIN - 1
EPS_NORM = 1e-06
EPS_LAYER = 1e-05
LOG2E = 1.4426950408889634
MASK2 = 100.0 * LOG2E
CENTRE = 8.0
MESH = pl.DeviceIdType.MESH
F32 = jnp.float32
BF16 = jnp.bfloat16


def iota(shape, dim):
    return lax.broadcasted_iota(jnp.int32, shape, dim)


def coordinate(offset):
    scaled = offset / (WIN - 1) * 8.0
    magnitude = jnp.log(jnp.abs(scaled) + 1.0) * (LOG2E / 3.0)
    return jnp.where(scaled < 0.0, -magnitude, magnitude)


def split_two(x):
    hi = x.astype(BF16)
    return hi, (x - hi.astype(F32)).astype(BF16)


def bias_strips(block, w_in_ref, w_off_ref, w_out_ref, table_ref):
    hidden_width = w_in_ref.shape[2]
    w0 = w_in_ref[block, 0:1, :]
    w1 = w_in_ref[block, 1:2, :]
    shift = w_off_ref[block : block + 1, :]
    w_hi, w_lo = split_two(w_out_ref[block])
    u = coordinate((WIN - 1) - iota((2 * WIN, 1), 0).astype(F32))
    row_term = u * w0 + shift
    for part in range(2):
        e = iota((WIN, 1), 0).astype(F32) + float(part * WIN)
        col_term = coordinate((WIN - 1) - e) * w1
        for piece in range(2):
            rows = [
                jnp.maximum(row_term[i : i + 1, :] + col_term, 0.0)
                for i in range(piece * WIN, (piece + 1) * WIN)
            ]
            h_hi, h_lo = split_two(jnp.concatenate(rows, axis=0))
            dims = (((1,), (1,)), ((), ()))
            out = lax.dot_general(w_hi, h_hi, dims, preferred_element_type=F32)
            out = out + lax.dot_general(w_hi, h_lo, dims, preferred_element_type=F32)
            out = out + lax.dot_general(w_lo, h_hi, dims, preferred_element_type=F32)
            value = 16.0 * LOG2E / (1.0 + jnp.exp2(out * -LOG2E)) - CENTRE * LOG2E
            first = part * 512 + piece * 256
            table_ref[:, first : first + 256] = value


def bias_expand(table_ref, bias_ref, mask_add):
    b_row = iota((WIN, 512), 0)
    d_col = iota((WIN, 512), 1) % WIN
    near = d_col <= b_row

    @pl.loop(0, HEADS)
    def _(h):
        x1 = jnp.broadcast_to(table_ref[pl.ds(h, 1), 0:512], (WIN, 512))
        x2 = jnp.broadcast_to(table_ref[pl.ds(h, 1), 512:1024], (WIN, 512))
        r1 = pltpu.roll(x1, 512 - (WIN - 1), 1, stride=1, stride_axis=0)
        r2 = pltpu.roll(x2, 1, 1, stride=1, stride_axis=0)
        strip = jnp.where(near, r1, r2)
        for a in range(HALF):
            m = 7 - a
            rolled = strip if m == 0 else pltpu.roll(strip, 512 - 16 * m, 1)
            piece = rolled[:, 0:384]
            if mask_add is not None:
                piece = piece + mask_add
            bias_ref[h, a * WIN : (a + 1) * WIN, :] = piece


def project(block, x_rows, w_ref, shift_ref, sharp_ref, q_ref, k_ref, v_ref):
    channels = x_rows.shape[1]
    same = (iota((256, 256), 0) // HEAD_DIM == iota((256, 256), 1) // HEAD_DIM).astype(BF16)
    lane_head = iota((1, LANES), 1) // HEAD_DIM
    for piece in range(channels // 256):
        for kind in range(3):
            first = kind * channels + piece * 256
            z = jnp.dot(x_rows, w_ref[:, first : first + 256], preferred_element_type=F32)
            here = slice(piece * 256, piece * 256 + 256)
            if kind == 0:
                z = z + shift_ref[block, 0:1, here]
            if kind == 2:
                z = z + shift_ref[block, 1:2, here]
            else:
                total = jnp.dot((z * z).astype(BF16), same, preferred_element_type=F32)
                z = z * lax.rsqrt(total + EPS_NORM)
            for half in range(2):
                group = piece * 2 + half
                part = z[:, half * LANES : (half + 1) * LANES]
                if kind == 0:
                    scale = jnp.zeros((1, LANES), F32)
                    for j in range(PACK):
                        scale = jnp.where(lane_head == j, sharp_ref[block, group * PACK + j], scale)
                    part = part * (scale * LOG2E)
                target = (q_ref, k_ref, v_ref)[kind]
                target[group] = part.astype(BF16)


def attention(q_ref, k_ref, v_ref, bias_ref, ctx_ref):
    lane_head = iota((1, LANES), 1) // HEAD_DIM

    @pl.loop(0, HEADS // PACK)
    def _(g):
        q = q_ref[g]
        k = k_ref[g]
        v = v_ref[g]
        weights, values = [], []
        for j in range(PACK):
            own = (lane_head == j).astype(BF16)
            scores = lax.dot_general(
                q, k * own, (((1,), (1,)), ((), ())), preferred_element_type=F32
            )
            h = g * PACK + j
            top = jnp.exp2(scores[:128] + bias_ref[h, :, 128:384]).astype(BF16)
            low = jnp.exp2(scores[128:] + bias_ref[h, :, 0:256]).astype(BF16)
            weights.append(jnp.concatenate([top, low], axis=0))
            values.append(jnp.concatenate([v * own, jnp.broadcast_to(own, v.shape)], axis=1))
        both = jnp.dot(
            jnp.concatenate(weights, axis=1),
            jnp.concatenate(values, axis=0),
            preferred_element_type=F32,
        )
        ctx_ref[g] = (both[:, :LANES] / both[:, LANES:]).astype(BF16)


def mix_and_norm(block, x_rows, ctx_ref, w_ref, add_ref, gain_ref, shift_ref):
    groups = ctx_ref.shape[0]
    ctx = jnp.concatenate([ctx_ref[g] for g in range(groups)], axis=1)
    branch = jnp.dot(ctx, w_ref[...], preferred_element_type=F32) + add_ref[block : block + 1, :]
    branch = branch - jnp.mean(branch, axis=-1, keepdims=True)
    spread = jnp.mean(branch * branch, axis=-1, keepdims=True)
    normed = branch * lax.rsqrt(spread + EPS_LAYER)
    return x_rows.astype(F32) + normed * gain_ref[block : block + 1, :] + shift_ref[block : block + 1, :]


def quadrants(rows):
    channels = rows.shape[1]
    grid = rows.reshape(2, HALF, 2, HALF, channels)
    return [
        jnp.concatenate([grid[i, r, j] for r in range(HALF)], axis=0)
        for i in range(2)
        for j in range(2)
    ]


def from_quadrants(parts):
    channels = parts[0].shape[1]
    rows = []
    for i in range(2):
        for r in range(HALF):
            for j in range(2):
                rows.append(parts[2 * i + j][r * HALF : (r + 1) * HALF, :])
    return jnp.concatenate(rows, axis=0)


def body(
    ny,
    nx,
    x_ref,
    w_qkv_hbm,
    qv_shift_ref,
    sharp_ref,
    w_in_ref,
    w_off_ref,
    w_out_ref,
    w_mix_hbm,
    mix_add_ref,
    gain_ref,
    shift_ref,
    out_ref,
    w_qkv_ref,
    w_mix_ref,
    table_ref,
    bias_ref,
    q_ref,
    k_ref,
    v_ref,
    ctx_ref,
    send_ref,
    window_ref,
    back_ref,
    home_ref,
    w_sem,
    send_sem,
    recv_sem,
    back_send_sem,
    back_recv_sem,
):
    gy = lax.axis_index("gy")
    gx = lax.axis_index("gx")
    prev_y, next_y = lax.rem(gy + ny - 1, ny), lax.rem(gy + 1, ny)
    prev_x, next_x = lax.rem(gx + nx - 1, nx), lax.rem(gx + 1, nx)
    givers = {1: (gy, prev_x), 2: (prev_y, gx), 3: (prev_y, prev_x)}
    takers = {1: (gy, next_x), 2: (next_y, gx), 3: (next_y, next_x)}

    barrier = pltpu.get_barrier_semaphore()
    for device in list(givers.values()) + list(takers.values()):
        pl.semaphore_signal(barrier, inc=1, device_id=device, device_id_type=MESH)

    loads = []
    for block in range(2):
        loads.append(
            (
                pltpu.make_async_copy(w_qkv_hbm.at[block], w_qkv_ref.at[block], w_sem.at[2 * block]),
                pltpu.make_async_copy(w_mix_hbm.at[block], w_mix_ref.at[block], w_sem.at[2 * block + 1]),
            )
        )
    for pair in loads:
        pair[0].start()
        pair[1].start()

    bias_strips(0, w_in_ref, w_off_ref, w_out_ref, table_ref)
    bias_expand(table_ref, bias_ref, None)
    loads[0][0].wait()
    x = x_ref[...]
    project(0, x, w_qkv_ref.at[0], qv_shift_ref, sharp_ref, q_ref, k_ref, v_ref)
    attention(q_ref, k_ref, v_ref, bias_ref, ctx_ref)
    loads[0][1].wait()
    first = mix_and_norm(0, x, ctx_ref, w_mix_ref.at[0], mix_add_ref, gain_ref, shift_ref)
    parts = quadrants(first)
    window_ref[0] = parts[3].astype(BF16)
    send_ref[0] = parts[2].astype(BF16)
    send_ref[1] = parts[1].astype(BF16)
    send_ref[2] = parts[0].astype(BF16)
    pl.semaphore_wait(barrier, 6)
    out_copies = [
        pltpu.make_async_remote_copy(
            src_ref=send_ref.at[n - 1],
            dst_ref=window_ref.at[n],
            send_sem=send_sem.at[n - 1],
            recv_sem=recv_sem.at[n - 1],
            device_id=givers[n],
            device_id_type=MESH,
        )
        for n in (1, 2, 3)
    ]
    for copy in out_copies:
        copy.start()

    bias_strips(1, w_in_ref, w_off_ref, w_out_ref, table_ref)
    b_low = iota((WIN, 384), 0) < HALF
    lane = iota((WIN, 384), 1)
    d_low = lane % WIN < HALF
    col_differs = jnp.where(b_low != d_low, 1, 0) * (gx == nx - 1).astype(jnp.int32)
    row_differs = jnp.where((lane < 128) | (lane >= 256), 1, 0) * (gy == ny - 1).astype(jnp.int32)
    mask_add = jnp.where(col_differs + row_differs > 0, -MASK2, 0.0)
    bias_expand(table_ref, bias_ref, mask_add)
    loads[1][0].wait()
    for copy in out_copies:
        copy.wait()

    x = from_quadrants([window_ref[n].astype(F32) for n in range(4)]).astype(BF16)
    project(1, x, w_qkv_ref.at[1], qv_shift_ref, sharp_ref, q_ref, k_ref, v_ref)
    attention(q_ref, k_ref, v_ref, bias_ref, ctx_ref)
    loads[1][1].wait()
    second = mix_and_norm(1, x, ctx_ref, w_mix_ref.at[1], mix_add_ref, gain_ref, shift_ref)
    parts = quadrants(second)
    for n in (1, 2, 3):
        back_ref[n - 1] = parts[n].astype(BF16)
    back_copies = [
        pltpu.make_async_remote_copy(
            src_ref=back_ref.at[n - 1],
            dst_ref=home_ref.at[n - 1],
            send_sem=back_send_sem.at[n - 1],
            recv_sem=back_recv_sem.at[n - 1],
            device_id=takers[n],
            device_id_type=MESH,
        )
        for n in (1, 2, 3)
    ]
    for copy in back_copies:
        copy.start()
    for copy in back_copies:
        copy.wait()
    home = [home_ref[2].astype(F32), home_ref[1].astype(F32), home_ref[0].astype(F32), parts[0]]
    out_ref[...] = from_quadrants(home).astype(BF16)


def on_device(x, w_qkv, qv_shift, sharp, w_in, w_off, w_out, w_mix, mix_add, gain, shift):
    rows, cols, channels = x.shape
    groups = HEADS // PACK
    vmem = pl.BlockSpec(memory_space=pltpu.VMEM)
    smem = pl.BlockSpec(memory_space=pltpu.SMEM)
    hbm = pl.BlockSpec(memory_space=pl.ANY)
    kernel = functools.partial(body, lax.axis_size("gy"), lax.axis_size("gx"))
    out = pl.pallas_call(
        kernel,
        out_shape=jax.ShapeDtypeStruct((rows * cols, channels), BF16),
        in_specs=[vmem, hbm, vmem, smem, vmem, vmem, vmem, hbm, vmem, vmem, vmem],
        out_specs=vmem,
        scratch_shapes=[
            pltpu.VMEM(w_qkv.shape, BF16),
            pltpu.VMEM(w_mix.shape, BF16),
            pltpu.VMEM((HEADS, 1024), F32),
            pltpu.VMEM((HEADS, 128, 384), F32),
            pltpu.VMEM((groups, TOKENS, LANES), BF16),
            pltpu.VMEM((groups, TOKENS, LANES), BF16),
            pltpu.VMEM((groups, TOKENS, LANES), BF16),
            pltpu.VMEM((groups, TOKENS, LANES), BF16),
            pltpu.VMEM((3, QUARTER, channels), BF16),
            pltpu.VMEM((4, QUARTER, channels), BF16),
            pltpu.VMEM((3, QUARTER, channels), BF16),
            pltpu.VMEM((3, QUARTER, channels), BF16),
            pltpu.SemaphoreType.DMA((4,)),
            pltpu.SemaphoreType.DMA((3,)),
            pltpu.SemaphoreType.DMA((3,)),
            pltpu.SemaphoreType.DMA((3,)),
            pltpu.SemaphoreType.DMA((3,)),
        ],
        compiler_params=pltpu.CompilerParams(
            collective_id=0, has_side_effects=True, vmem_limit_bytes=56 * 1024 * 1024
        ),
    )(
        x.reshape(rows * cols, channels),
        w_qkv,
        qv_shift,
        sharp,
        w_in,
        w_off,
        jnp.swapaxes(w_out, 1, 2),
        w_mix,
        mix_add,
        gain,
        shift,
    )
    return out.reshape(rows, cols, channels)


def solution(mesh):
    in_specs = (P("gy", "gx", None), P(), P(), P(), P(), P(), P(), P(), P(), P(), P())
    return jax.shard_map(
        on_device, mesh=mesh, in_specs=in_specs, out_specs=P("gy", "gx", None), check_vma=False
    )
```

profile of v0, /device:TPU:0, one launch (start us, length us, event | category | flops | bytes accessed | tf_op | source)
XLA Modules:
  0.0 38.3 jit_solution(6908743609187515498)
XLA Ops:
  0.0 36.5 %shard_map.109 = bf16[256,768]{1,0:T(8,128)(2,1)} custom-call(bf16[256,768]{1,0:T(8,128)(2,1)} %bitcast.4, bf16[2,768,2304]{2,1,0:T(8,128)(2,1)} %w_qkv_hbm.1, f32[2,2,768]{2,1,0:T(2,128)} %qv_shift_ref.1, f32[2,24]{1,0:T(2,128)} %sharp_ref.1, f32[2,2,512]{2,1,0:T(2,128)} %w_in_ref.1, f32[2,512]{1,0:T(2,128)} %w_off_ref.1, f32[2,24,512]{2,1,0:T(8,128)} %bitcast.5, ...), custom_call_target="tpu_custom_call" | custom-call | tf_op jit(solution)/shard_map/pallas_call | solution.py:306
  36.5 1.8 %copy.13 = bf16[16,16,768]{2,1,0:T(8,128)(2,1)} copy(bf16[16,16,768]{2,1,0:T(8,128)(2,1)} %bitcast.3) | data formatting | bytes 786432
where the time goes:
time: 38.5 us; the launch traced here: 38.3 us
  Pallas kernels  36.5 us (95%)
  local copies, waits for them, and re-layouts  1.77 us (5%)
    pallas_call x1, Pallas kernels, on_device(): pl.pallas_call(kernel, out_shape=jax.ShapeDtypeStruct((rows * cols, chann...  36.5 us
    unnamed x1, local copies, waits for them, and re-layouts  1.77 us

commit v1 on v0

--- a/solution.py
+++ b/solution.py
@@ -21,6 +21,7 @@
 LOG2E = 1.4426950408889634
 MASK2 = 100.0 * LOG2E
 CENTRE = 8.0
+FIXED = 4095.0
 MESH = pl.DeviceIdType.MESH
 F32 = jnp.float32
 BF16 = jnp.bfloat16
@@ -42,50 +43,58 @@
 
 
 def bias_strips(block, w_in_ref, w_off_ref, w_out_ref, table_ref):
-    hidden_width = w_in_ref.shape[2]
     w0 = w_in_ref[block, 0:1, :]
     w1 = w_in_ref[block, 1:2, :]
     shift = w_off_ref[block : block + 1, :]
-    w_hi, w_lo = split_two(w_out_ref[block])
+    w_out = w_out_ref[block]
+    heads = w_out.shape[0]
+    w_hi, w_lo = split_two(w_out)
+    w_both = jnp.concatenate([w_hi.astype(F32), w_lo.astype(F32)], axis=0).astype(BF16)
     u = coordinate((WIN - 1) - iota((2 * WIN, 1), 0).astype(F32))
     row_term = u * w0 + shift
-    for part in range(2):
-        e = iota((WIN, 1), 0).astype(F32) + float(part * WIN)
-        col_term = coordinate((WIN - 1) - e) * w1
-        for piece in range(2):
-            rows = [
-                jnp.maximum(row_term[i : i + 1, :] + col_term, 0.0)
-                for i in range(piece * WIN, (piece + 1) * WIN)
-            ]
+    dims = (((1,), (1,)), ((), ()))
+    for piece in range(2):
+        fixed = []
+        for part in range(2):
+            e = iota((WIN, 1), 0).astype(F32) + float(part * WIN)
+            col_term = coordinate((WIN - 1) - e) * w1
+            rows = []
+            for i in range(piece * WIN, (piece + 1) * WIN):
+                at = (i - part) % (2 * WIN)
+                rows.append(jnp.maximum(row_term[at : at + 1, :] + col_term, 0.0))
             h_hi, h_lo = split_two(jnp.concatenate(rows, axis=0))
-            dims = (((1,), (1,)), ((), ()))
-            out = lax.dot_general(w_hi, h_hi, dims, preferred_element_type=F32)
-            out = out + lax.dot_general(w_hi, h_lo, dims, preferred_element_type=F32)
-            out = out + lax.dot_general(w_lo, h_hi, dims, preferred_element_type=F32)
-            value = 16.0 * LOG2E / (1.0 + jnp.exp2(out * -LOG2E)) - CENTRE * LOG2E
-            first = part * 512 + piece * 256
-            table_ref[:, first : first + 256] = value
+            both = lax.dot_general(w_both, h_hi, dims, preferred_element_type=F32)
+            out = lax.dot_general(w_hi, h_lo, dims, preferred_element_type=F32)
+            out = out + both[:heads] + both[heads:]
+            value = 16.0 / (1.0 + jnp.exp2(out * -LOG2E)) - CENTRE
+            fixed.append(jnp.round(value * FIXED).astype(jnp.int32))
+        table_ref[:, piece * 256 : piece * 256 + 256] = (fixed[0] << 16) | (fixed[1] & 0xFFFF)
+
+
+def expand_head(table_ref, bias_ref, h, mask_add):
+    b_row = iota((WIN, 512), 0)
+    near = iota((WIN, 512), 1) % WIN <= b_row
+    x = jnp.broadcast_to(table_ref[pl.ds(h, 1), :], (WIN, 512))
+    r = pltpu.roll(x, 512 - (WIN - 1), 1, stride=1, stride_axis=0)
+    strip = jnp.where(near, r, r << 16)
+    pair = (strip[:HALF] & -65536) | lax.shift_right_logical(strip[HALF:], 16)
+    for a in range(HALF):
+        m = 7 - a
+        rolled = pair if m == 0 else pltpu.roll(pair, 512 - 16 * m, 1)
+        rolled = rolled[:, 0:384]
+        first = (rolled >> 16).astype(F32) * (LOG2E / FIXED)
+        second = ((rolled << 16) >> 16).astype(F32) * (LOG2E / FIXED)
+        if mask_add is not None:
+            first = first + mask_add[:HALF]
+            second = second + mask_add[HALF:]
+        bias_ref[h, a * WIN : a * WIN + HALF, :] = first
+        bias_ref[h, a * WIN + HALF : (a + 1) * WIN, :] = second
 
 
 def bias_expand(table_ref, bias_ref, mask_add):
-    b_row = iota((WIN, 512), 0)
-    d_col = iota((WIN, 512), 1) % WIN
-    near = d_col <= b_row
-
-    @pl.loop(0, HEADS)
+    @pl.loop(0, HEADS, unroll=8)
     def _(h):
-        x1 = jnp.broadcast_to(table_ref[pl.ds(h, 1), 0:512], (WIN, 512))
-        x2 = jnp.broadcast_to(table_ref[pl.ds(h, 1), 512:1024], (WIN, 512))
-        r1 = pltpu.roll(x1, 512 - (WIN - 1), 1, stride=1, stride_axis=0)
-        r2 = pltpu.roll(x2, 1, 1, stride=1, stride_axis=0)
-        strip = jnp.where(near, r1, r2)
-        for a in range(HALF):
-            m = 7 - a
-            rolled = strip if m == 0 else pltpu.roll(strip, 512 - 16 * m, 1)
-            piece = rolled[:, 0:384]
-            if mask_add is not None:
-                piece = piece + mask_add
-            bias_ref[h, a * WIN : (a + 1) * WIN, :] = piece
+        expand_head(table_ref, bias_ref, h, mask_add)
 
 
 def project(block, x_rows, w_ref, shift_ref, sharp_ref, q_ref, k_ref, v_ref):
@@ -119,7 +128,7 @@
 def attention(q_ref, k_ref, v_ref, bias_ref, ctx_ref):
     lane_head = iota((1, LANES), 1) // HEAD_DIM
 
-    @pl.loop(0, HEADS // PACK)
+    @pl.loop(0, HEADS // PACK, unroll=HEADS // PACK)
     def _(g):
         q = q_ref[g]
         k = k_ref[g]
@@ -199,7 +208,6 @@
     send_ref,
     window_ref,
     back_ref,
-    home_ref,
     w_sem,
     send_sem,
     recv_sem,
@@ -275,14 +283,14 @@
     loads[1][1].wait()
     second = mix_and_norm(1, x, ctx_ref, w_mix_ref.at[1], mix_add_ref, gain_ref, shift_ref)
     parts = quadrants(second)
-    for n in (1, 2, 3):
-        back_ref[n - 1] = parts[n].astype(BF16)
+    for n in range(4):
+        back_ref[n] = parts[n].astype(BF16)
     back_copies = [
         pltpu.make_async_remote_copy(
-            src_ref=back_ref.at[n - 1],
-            dst_ref=home_ref.at[n - 1],
-            send_sem=back_send_sem.at[n - 1],
-            recv_sem=back_recv_sem.at[n - 1],
+            src_ref=back_ref.at[n],
+            dst_ref=out_ref.at[3 - n],
+            send_sem=back_send_sem.at[n],
+            recv_sem=back_recv_sem.at[n],
             device_id=takers[n],
             device_id_type=MESH,
         )
@@ -290,10 +298,11 @@
     ]
     for copy in back_copies:
         copy.start()
+    keep = pltpu.make_async_copy(back_ref.at[0], out_ref.at[3], back_send_sem.at[0])
+    keep.start()
     for copy in back_copies:
         copy.wait()
-    home = [home_ref[2].astype(F32), home_ref[1].astype(F32), home_ref[0].astype(F32), parts[0]]
-    out_ref[...] = from_quadrants(home).astype(BF16)
+    keep.wait()
 
 
 def on_device(x, w_qkv, qv_shift, sharp, w_in, w_off, w_out, w_mix, mix_add, gain, shift):
@@ -305,13 +314,13 @@
     kernel = functools.partial(body, lax.axis_size("gy"), lax.axis_size("gx"))
     out = pl.pallas_call(
         kernel,
-        out_shape=jax.ShapeDtypeStruct((rows * cols, channels), BF16),
+        out_shape=jax.ShapeDtypeStruct((4, QUARTER, channels), BF16),
         in_specs=[vmem, hbm, vmem, smem, vmem, vmem, vmem, hbm, vmem, vmem, vmem],
-        out_specs=vmem,
+        out_specs=hbm,
         scratch_shapes=[
             pltpu.VMEM(w_qkv.shape, BF16),
             pltpu.VMEM(w_mix.shape, BF16),
-            pltpu.VMEM((HEADS, 1024), F32),
+            pltpu.VMEM((HEADS, 512), jnp.int32),
             pltpu.VMEM((HEADS, 128, 384), F32),
             pltpu.VMEM((groups, TOKENS, LANES), BF16),
             pltpu.VMEM((groups, TOKENS, LANES), BF16),
@@ -319,13 +328,12 @@
             pltpu.VMEM((groups, TOKENS, LANES), BF16),
             pltpu.VMEM((3, QUARTER, channels), BF16),
             pltpu.VMEM((4, QUARTER, channels), BF16),
-            pltpu.VMEM((3, QUARTER, channels), BF16),
-            pltpu.VMEM((3, QUARTER, channels), BF16),
+            pltpu.VMEM((4, QUARTER, channels), BF16),
             pltpu.SemaphoreType.DMA((4,)),
             pltpu.SemaphoreType.DMA((3,)),
             pltpu.SemaphoreType.DMA((3,)),
-            pltpu.SemaphoreType.DMA((3,)),
-            pltpu.SemaphoreType.DMA((3,)),
+            pltpu.SemaphoreType.DMA((4,)),
+            pltpu.SemaphoreType.DMA((4,)),
         ],
         compiler_params=pltpu.CompilerParams(
             collective_id=0, has_side_effects=True, vmem_limit_bytes=56 * 1024 * 1024
@@ -343,6 +351,7 @@
         gain,
         shift,
     )
+    out = out.reshape(2, 2, HALF, HALF, channels).transpose(0, 2, 1, 3, 4)
     return out.reshape(rows, cols, channels)
 
 

time: 38.5 us -> 30.3 us (0.79)
  Pallas kernels: 36.5 us -> 28.3 us
    pallas_call x1, Pallas kernels: 36.5 us -> 28.3 us  [on_device(): pl.pallas_call(kernel, out_shape=jax.ShapeDtypeStruct((4, QUARTER, channe...]
    transpose x0 -> x1, local copies, waits for them, and re-layouts: none -> 1.77 us  [on_device(): out = out.reshape(2, 2, HALF, HALF, channels).transpose(0, 2, 1, 3, 4)]
    unnamed x1 -> x0, local copies, waits for them, and re-layouts: 1.77 us -> none
where the time goes in v1:
time: 30.3 us; the launch traced here: 30.1 us
  Pallas kernels  28.3 us (93%)
  local copies, waits for them, and re-layouts  1.77 us (6%)
    pallas_call x1, Pallas kernels, on_device(): pl.pallas_call(kernel, out_shape=jax.ShapeDtypeStruct((4, QUARTER, channe...  28.3 us
    transpose x1, local copies, waits for them, and re-layouts, on_device(): out = out.reshape(2, 2, HALF, HALF, channels).transpose(0, 2, 1, 3, 4)  1.77 us

profile of v1, /device:TPU:0, one launch (start us, length us, event | category | flops | bytes accessed | tf_op | source)
XLA Modules:
  0.0 30.1 jit_solution(6636660101375396155)
XLA Ops:
  0.0 28.3 %shard_map.109 = bf16[4,64,768]{2,1,0:T(8,128)(2,1)} custom-call(bf16[256,768]{1,0:T(8,128)(2,1)} %bitcast.7, bf16[2,768,2304]{2,1,0:T(8,128)(2,1)} %w_qkv_hbm.1, f32[2,2,768]{2,1,0:T(2,128)} %qv_shift_ref.1, f32[2,24]{1,0:T(2,128)} %sharp_ref.1, f32[2,2,512]{2,1,0:T(2,128)} %w_in_ref.1, f32[2,512]{1,0:T(2,128)} %w_off_ref.1, f32[2,24,512]{2,1,0:T(8,128)} %bitcast.8, ...), custom_call_target="tpu_custom_call" | custom-call | tf_op jit(solution)/shard_map/pallas_call | solution.py:315
  28.4 1.8 %copy.12 = bf16[2,8,2,8,768]{4,3,2,1,0:T(8,128)(2,1)} copy(bf16[2,8,2,8,768]{4,3,1,2,0:T(8,128)(2,1)} %bitcast.6) | data formatting | bytes 786432 | tf_op jit(solution)/shard_map/transpose | solution.py:354

commit v2 on v1

--- a/solution.py
+++ b/solution.py
@@ -97,7 +97,7 @@
         expand_head(table_ref, bias_ref, h, mask_add)
 
 
-def project(block, x_rows, w_ref, shift_ref, sharp_ref, q_ref, k_ref, v_ref):
+def project(block, x_rows, w_ref, shift_ref, sharp_ref, q_ref, k_ref, v_ref, beside=None):
     channels = x_rows.shape[1]
     same = (iota((256, 256), 0) // HEAD_DIM == iota((256, 256), 1) // HEAD_DIM).astype(BF16)
     lane_head = iota((1, LANES), 1) // HEAD_DIM
@@ -123,14 +123,18 @@
                     part = part * (scale * LOG2E)
                 target = (q_ref, k_ref, v_ref)[kind]
                 target[group] = part.astype(BF16)
-
-
-def attention(q_ref, k_ref, v_ref, bias_ref, ctx_ref):
+            if beside is not None:
+                beside(piece * 3 + kind)
+
+
+def attention(half, q_ref, k_ref, v_ref, bias_ref, ctx_ref):
     lane_head = iota((1, LANES), 1) // HEAD_DIM
+    first = half * (TOKENS // 2)
+    lanes = slice(128, 384) if half == 0 else slice(0, 256)
 
     @pl.loop(0, HEADS // PACK, unroll=HEADS // PACK)
     def _(g):
-        q = q_ref[g]
+        q = q_ref[g, first : first + TOKENS // 2, :]
         k = k_ref[g]
         v = v_ref[g]
         weights, values = [], []
@@ -140,36 +144,31 @@
                 q, k * own, (((1,), (1,)), ((), ())), preferred_element_type=F32
             )
             h = g * PACK + j
-            top = jnp.exp2(scores[:128] + bias_ref[h, :, 128:384]).astype(BF16)
-            low = jnp.exp2(scores[128:] + bias_ref[h, :, 0:256]).astype(BF16)
-            weights.append(jnp.concatenate([top, low], axis=0))
+            weights.append(jnp.exp2(scores + bias_ref[h, :, lanes]).astype(BF16))
             values.append(jnp.concatenate([v * own, jnp.broadcast_to(own, v.shape)], axis=1))
         both = jnp.dot(
             jnp.concatenate(weights, axis=1),
             jnp.concatenate(values, axis=0),
             preferred_element_type=F32,
         )
-        ctx_ref[g] = (both[:, :LANES] / both[:, LANES:]).astype(BF16)
-
-
-def mix_and_norm(block, x_rows, ctx_ref, w_ref, add_ref, gain_ref, shift_ref):
+        ctx_ref[g, first : first + TOKENS // 2, :] = (both[:, :LANES] / both[:, LANES:]).astype(BF16)
+
+
+def mix_and_norm(half, block, x_rows, ctx_ref, w_ref, add_ref, gain_ref, shift_ref):
     groups = ctx_ref.shape[0]
-    ctx = jnp.concatenate([ctx_ref[g] for g in range(groups)], axis=1)
+    here = slice(half * (TOKENS // 2), (half + 1) * (TOKENS // 2))
+    ctx = jnp.concatenate([ctx_ref[g, here, :] for g in range(groups)], axis=1)
     branch = jnp.dot(ctx, w_ref[...], preferred_element_type=F32) + add_ref[block : block + 1, :]
     branch = branch - jnp.mean(branch, axis=-1, keepdims=True)
     spread = jnp.mean(branch * branch, axis=-1, keepdims=True)
     normed = branch * lax.rsqrt(spread + EPS_LAYER)
-    return x_rows.astype(F32) + normed * gain_ref[block : block + 1, :] + shift_ref[block : block + 1, :]
-
-
-def quadrants(rows):
-    channels = rows.shape[1]
-    grid = rows.reshape(2, HALF, 2, HALF, channels)
-    return [
-        jnp.concatenate([grid[i, r, j] for r in range(HALF)], axis=0)
-        for i in range(2)
-        for j in range(2)
-    ]
+    x_half = x_rows[here, :].astype(F32)
+    return x_half + normed * gain_ref[block : block + 1, :] + shift_ref[block : block + 1, :]
+
+
+def two_sides(rows):
+    grid = rows.reshape(HALF, 2, HALF, rows.shape[1])
+    return [jnp.concatenate([grid[r, j] for r in range(HALF)], axis=0) for j in range(2)]
 
 
 def from_quadrants(parts):
@@ -238,21 +237,16 @@
         pair[1].start()
 
     bias_strips(0, w_in_ref, w_off_ref, w_out_ref, table_ref)
-    bias_expand(table_ref, bias_ref, None)
+
+    def some_bias(step):
+        for h in range(step * HEADS // 9, (step + 1) * HEADS // 9):
+            expand_head(table_ref, bias_ref, h, None)
+
     loads[0][0].wait()
     x = x_ref[...]
-    project(0, x, w_qkv_ref.at[0], qv_shift_ref, sharp_ref, q_ref, k_ref, v_ref)
-    attention(q_ref, k_ref, v_ref, bias_ref, ctx_ref)
-    loads[0][1].wait()
-    first = mix_and_norm(0, x, ctx_ref, w_mix_ref.at[0], mix_add_ref, gain_ref, shift_ref)
-    parts = quadrants(first)
-    window_ref[0] = parts[3].astype(BF16)
-    send_ref[0] = parts[2].astype(BF16)
-    send_ref[1] = parts[1].astype(BF16)
-    send_ref[2] = parts[0].astype(BF16)
-    pl.semaphore_wait(barrier, 6)
-    out_copies = [
-        pltpu.make_async_remote_copy(
+    project(0, x, w_qkv_ref.at[0], qv_shift_ref, sharp_ref, q_ref, k_ref, v_ref, some_bias)
+    out_copies = {
+        n: pltpu.make_async_remote_copy(
             src_ref=send_ref.at[n - 1],
             dst_ref=window_ref.at[n],
             send_sem=send_sem.at[n - 1],
@@ -261,9 +255,21 @@
             device_id_type=MESH,
         )
         for n in (1, 2, 3)
-    ]
-    for copy in out_copies:
-        copy.start()
+    }
+    attention(0, q_ref, k_ref, v_ref, bias_ref, ctx_ref)
+    loads[0][1].wait()
+    mixed = (0, x, ctx_ref, w_mix_ref.at[0], mix_add_ref, gain_ref, shift_ref)
+    left, right = two_sides(mix_and_norm(0, *mixed))
+    send_ref[2] = left.astype(BF16)
+    send_ref[1] = right.astype(BF16)
+    pl.semaphore_wait(barrier, 6)
+    out_copies[3].start()
+    out_copies[2].start()
+    attention(1, q_ref, k_ref, v_ref, bias_ref, ctx_ref)
+    left, right = two_sides(mix_and_norm(1, *mixed))
+    send_ref[0] = left.astype(BF16)
+    out_copies[1].start()
+    window_ref[0] = right.astype(BF16)
 
     bias_strips(1, w_in_ref, w_off_ref, w_out_ref, table_ref)
     b_low = iota((WIN, 384), 0) < HALF
@@ -274,19 +280,13 @@
     mask_add = jnp.where(col_differs + row_differs > 0, -MASK2, 0.0)
     bias_expand(table_ref, bias_ref, mask_add)
     loads[1][0].wait()
-    for copy in out_copies:
+    for copy in out_copies.values():
         copy.wait()
 
     x = from_quadrants([window_ref[n].astype(F32) for n in range(4)]).astype(BF16)
     project(1, x, w_qkv_ref.at[1], qv_shift_ref, sharp_ref, q_ref, k_ref, v_ref)
-    attention(q_ref, k_ref, v_ref, bias_ref, ctx_ref)
-    loads[1][1].wait()
-    second = mix_and_norm(1, x, ctx_ref, w_mix_ref.at[1], mix_add_ref, gain_ref, shift_ref)
-    parts = quadrants(second)
-    for n in range(4):
-        back_ref[n] = parts[n].astype(BF16)
-    back_copies = [
-        pltpu.make_async_remote_copy(
+    back_copies = {
+        n: pltpu.make_async_remote_copy(
             src_ref=back_ref.at[n],
             dst_ref=out_ref.at[3 - n],
             send_sem=back_send_sem.at[n],
@@ -295,12 +295,23 @@
             device_id_type=MESH,
         )
         for n in (1, 2, 3)
-    ]
-    for copy in back_copies:
-        copy.start()
+    }
+    attention(1, q_ref, k_ref, v_ref, bias_ref, ctx_ref)
+    loads[1][1].wait()
+    mixed = (1, x, ctx_ref, w_mix_ref.at[1], mix_add_ref, gain_ref, shift_ref)
+    left, right = two_sides(mix_and_norm(1, *mixed))
+    back_ref[3] = right.astype(BF16)
+    back_copies[3].start()
+    back_ref[2] = left.astype(BF16)
+    back_copies[2].start()
+    attention(0, q_ref, k_ref, v_ref, bias_ref, ctx_ref)
+    left, right = two_sides(mix_and_norm(0, *mixed))
+    back_ref[1] = right.astype(BF16)
+    back_copies[1].start()
+    back_ref[0] = left.astype(BF16)
     keep = pltpu.make_async_copy(back_ref.at[0], out_ref.at[3], back_send_sem.at[0])
     keep.start()
-    for copy in back_copies:
+    for copy in back_copies.values():
         copy.wait()
     keep.wait()
 

time: 30.3 us -> 28.2 us (0.931)
  Pallas kernels: 28.3 us -> 26.3 us
    pallas_call x1, Pallas kernels: 28.3 us -> 26.3 us  [on_device(): pl.pallas_call(kernel, out_shape=jax.ShapeDtypeStruct((4, QUARTER, channe...]
where the time goes in v2:
time: 28.2 us; the launch traced here: 28 us
  Pallas kernels  26.3 us (93%)
  local copies, waits for them, and re-layouts  1.77 us (6%)
    pallas_call x1, Pallas kernels, on_device(): pl.pallas_call(kernel, out_shape=jax.ShapeDtypeStruct((4, QUARTER, channe...  26.3 us
    transpose x1, local copies, waits for them, and re-layouts, on_device(): out = out.reshape(2, 2, HALF, HALF, channels).transpose(0, 2, 1, 3, 4)  1.77 us

profile of v2, /device:TPU:0, one launch (start us, length us, event | category | flops | bytes accessed | tf_op | source)
XLA Modules:
  0.0 28.0 jit_solution(13156415980509140299)
XLA Ops:
  0.0 26.3 %shard_map.109 = bf16[4,64,768]{2,1,0:T(8,128)(2,1)} custom-call(bf16[256,768]{1,0:T(8,128)(2,1)} %bitcast.7, bf16[2,768,2304]{2,1,0:T(8,128)(2,1)} %w_qkv_hbm.1, f32[2,2,768]{2,1,0:T(2,128)} %qv_shift_ref.1, f32[2,24]{1,0:T(2,128)} %sharp_ref.1, f32[2,2,512]{2,1,0:T(2,128)} %w_in_ref.1, f32[2,512]{1,0:T(2,128)} %w_off_ref.1, f32[2,24,512]{2,1,0:T(8,128)} %bitcast.8, ...), custom_call_target="tpu_custom_call" | custom-call | tf_op jit(solution)/shard_map/pallas_call | solution.py:326
  26.3 1.8 %copy.12 = bf16[2,8,2,8,768]{4,3,2,1,0:T(8,128)(2,1)} copy(bf16[2,8,2,8,768]{4,3,1,2,0:T(8,128)(2,1)} %bitcast.6) | data formatting | bytes 786432 | tf_op jit(solution)/shard_map/transpose | solution.py:365

commit v3 on v2

--- a/solution.py
+++ b/solution.py
@@ -152,6 +152,33 @@
             preferred_element_type=F32,
         )
         ctx_ref[g, first : first + TOKENS // 2, :] = (both[:, :LANES] / both[:, LANES:]).astype(BF16)
+
+
+def attention_all(q_ref, k_ref, v_ref, bias_ref, ctx_ref):
+    lane_head = iota((1, LANES), 1) // HEAD_DIM
+
+    @pl.loop(0, HEADS // PACK, unroll=HEADS // PACK)
+    def _(g):
+        q = q_ref[g]
+        k = k_ref[g]
+        v = v_ref[g]
+        weights, values = [], []
+        for j in range(PACK):
+            own = (lane_head == j).astype(BF16)
+            scores = lax.dot_general(
+                q, k * own, (((1,), (1,)), ((), ())), preferred_element_type=F32
+            )
+            h = g * PACK + j
+            top = jnp.exp2(scores[:128] + bias_ref[h, :, 128:384]).astype(BF16)
+            low = jnp.exp2(scores[128:] + bias_ref[h, :, 0:256]).astype(BF16)
+            weights.append(jnp.concatenate([top, low], axis=0))
+            values.append(jnp.concatenate([v * own, jnp.broadcast_to(own, v.shape)], axis=1))
+        both = jnp.dot(
+            jnp.concatenate(weights, axis=1),
+            jnp.concatenate(values, axis=0),
+            preferred_element_type=F32,
+        )
+        ctx_ref[g] = (both[:, :LANES] / both[:, LANES:]).astype(BF16)
 
 
 def mix_and_norm(half, block, x_rows, ctx_ref, w_ref, add_ref, gain_ref, shift_ref):
@@ -232,9 +259,7 @@
                 pltpu.make_async_copy(w_mix_hbm.at[block], w_mix_ref.at[block], w_sem.at[2 * block + 1]),
             )
         )
-    for pair in loads:
-        pair[0].start()
-        pair[1].start()
+    loads[0][0].start()
 
     bias_strips(0, w_in_ref, w_off_ref, w_out_ref, table_ref)
 
@@ -243,6 +268,9 @@
             expand_head(table_ref, bias_ref, h, None)
 
     loads[0][0].wait()
+    loads[0][1].start()
+    loads[1][0].start()
+    loads[1][1].start()
     x = x_ref[...]
     project(0, x, w_qkv_ref.at[0], qv_shift_ref, sharp_ref, q_ref, k_ref, v_ref, some_bias)
     out_copies = {
@@ -256,7 +284,7 @@
         )
         for n in (1, 2, 3)
     }
-    attention(0, q_ref, k_ref, v_ref, bias_ref, ctx_ref)
+    attention_all(q_ref, k_ref, v_ref, bias_ref, ctx_ref)
     loads[0][1].wait()
     mixed = (0, x, ctx_ref, w_mix_ref.at[0], mix_add_ref, gain_ref, shift_ref)
     left, right = two_sides(mix_and_norm(0, *mixed))
@@ -265,7 +293,6 @@
     pl.semaphore_wait(barrier, 6)
     out_copies[3].start()
     out_copies[2].start()
-    attention(1, q_ref, k_ref, v_ref, bias_ref, ctx_ref)
     left, right = two_sides(mix_and_norm(1, *mixed))
     send_ref[0] = left.astype(BF16)
     out_copies[1].start()

time: 28.2 us -> 29.2 us (1.035)
  Pallas kernels: 26.3 us -> 27.2 us
    pallas_call x1, Pallas kernels: 26.3 us -> 27.2 us  [on_device(): pl.pallas_call(kernel, out_shape=jax.ShapeDtypeStruct((4, QUARTER, channe...]
where the time goes in v3:
time: 29.2 us; the launch traced here: 29 us
  Pallas kernels  27.2 us (93%)
  local copies, waits for them, and re-layouts  1.77 us (6%)
    pallas_call x1, Pallas kernels, on_device(): pl.pallas_call(kernel, out_shape=jax.ShapeDtypeStruct((4, QUARTER, channe...  27.2 us
    transpose x1, local copies, waits for them, and re-layouts, on_device(): out = out.reshape(2, 2, HALF, HALF, channels).transpose(0, 2, 1, 3, 4)  1.77 us

profile of v3, /device:TPU:0, one launch (start us, length us, event | category | flops | bytes accessed | tf_op | source)
XLA Modules:
  0.0 29.0 jit_solution(14682091720246871864)
XLA Ops:
  0.0 27.2 %shard_map.109 = bf16[4,64,768]{2,1,0:T(8,128)(2,1)} custom-call(bf16[256,768]{1,0:T(8,128)(2,1)} %bitcast.7, bf16[2,768,2304]{2,1,0:T(8,128)(2,1)} %w_qkv_hbm.1, f32[2,2,768]{2,1,0:T(2,128)} %qv_shift_ref.1, f32[2,24]{1,0:T(2,128)} %sharp_ref.1, f32[2,2,512]{2,1,0:T(2,128)} %w_in_ref.1, f32[2,512]{1,0:T(2,128)} %w_off_ref.1, f32[2,24,512]{2,1,0:T(8,128)} %bitcast.8, ...), custom_call_target="tpu_custom_call" | custom-call | tf_op jit(solution)/shard_map/pallas_call | solution.py:353
  27.2 1.8 %copy.12 = bf16[2,8,2,8,768]{4,3,2,1,0:T(8,128)(2,1)} copy(bf16[2,8,2,8,768]{4,3,1,2,0:T(8,128)(2,1)} %bitcast.6) | data formatting | bytes 786432 | tf_op jit(solution)/shard_map/transpose | solution.py:392
